TPU v7x, 512 devices: a whole 4x8x8 slice. The times are simulated.
512 devices in a mesh: dp: 2 (over z_lo), gx: 8 (over y), gy: 4 (over x), gz: 8 (over z_hi, core).
Axes of the slice: x: 4, y: 8, z: 8 (z_hi: 4, z_lo: 2; z = z_hi * 2 + z_lo), core: 2. Of those that a mesh axis runs over, the one named last changes fastest.
Arguments:
- tokens: bfloat16 [1024, 4096], P(('dp', 'gx', 'gy'), 'gz'), may hold values from -6 to 6
- gate_weight: bfloat16 [4096, 14848], P('gz', ('gx', 'gy')), may hold values from -0.09375 to 0.09375
- up_weight: bfloat16 [4096, 14848], P('gz', ('gx', 'gy')), may hold values from -0.09375 to 0.09375
- down_weight: bfloat16 [14848, 4096], P(('gx', 'gy'), 'gz'), may hold values from -0.046875 to 0.046875
- out_grad: bfloat16 [1024, 4096], P(('dp', 'gx', 'gy'), 'gz'), may hold values from -6 to 6
Outputs:
- output: bfloat16 [1024, 4096], P(('dp', 'gx', 'gy'), 'gz')
- input_grad: bfloat16 [1024, 4096], P(('dp', 'gx', 'gy'), 'gz')
- gate_grad: bfloat16 [4096, 14848], P('gz', ('gx', 'gy'))
- up_grad: bfloat16 [4096, 14848], P('gz', ('gx', 'gy'))
- down_grad: bfloat16 [14848, 4096], P(('gx', 'gy'), 'gz')
All inputs are finite; a program needn't handle non-finite values.
Results may differ from a plain program's by a relative error of at most 0.03.
Values may be sent and summed in bfloat16 or wider, within the bound.
A program may use at most 64 MiB of HBM per device.

v0:
```python
import jax
import jax.numpy as jnp
from jax import lax
from jax.sharding import PartitionSpec as P


def body(tokens, gate_weight, up_weight, down_weight, out_grad):
    tok_set, grad_set = (
        lax.all_gather(tokens, "gx", axis=0, tiled=True),
        lax.all_gather(out_grad, "gx", axis=0, tiled=True),
    )
    tok_all, grad_all = (
        lax.all_gather(tok_set, "gy", axis=0, tiled=True),
        lax.all_gather(grad_set, "gy", axis=0, tiled=True),
    )
    back_dims = (((1,), (1,)), ((), ()))
    gate_full, up_full = (
        lax.all_gather(gate_weight, "gy", axis=1, tiled=True),
        lax.all_gather(up_weight, "gy", axis=1, tiled=True),
    )
    gate_part = jnp.dot(tok_set, gate_full, preferred_element_type=jnp.float32)
    up_part = jnp.dot(tok_set, up_full, preferred_element_type=jnp.float32)
    gate_val, up_val = (
        lax.psum_scatter(
            gate_part.astype(jnp.bfloat16), "gz", scatter_dimension=0, tiled=True
        ).astype(jnp.float32),
        lax.psum_scatter(
            up_part.astype(jnp.bfloat16), "gz", scatter_dimension=0, tiled=True
        ).astype(jnp.float32),
    )
    gate_sig = jax.nn.sigmoid(gate_val)
    gate_act = gate_val * gate_sig
    hidden = (gate_act * up_val).astype(jnp.bfloat16)
    hidden_set = lax.all_gather(hidden, "gz", axis=0, tiled=True)
    down_full = lax.all_gather(down_weight, "gy", axis=0, tiled=True)
    rows_now = hidden_set
    output = lax.psum_scatter(
        jnp.dot(rows_now, down_full, preferred_element_type=jnp.float32).astype(jnp.bfloat16),
        "gx",
        scatter_dimension=0,
        tiled=True,
    )
    rows_now = grad_set
    hid_grad = lax.psum_scatter(
        lax.dot_general(rows_now, down_full, back_dims, preferred_element_type=jnp.float32).astype(
            jnp.bfloat16
        ),
        "gz",
        scatter_dimension=0,
        tiled=True,
    ).astype(jnp.float32)
    gate_delta = (hid_grad * up_val * gate_sig * (1.0 + gate_val * (1.0 - gate_sig))).astype(
        jnp.bfloat16
    )
    up_delta = (hid_grad * gate_act).astype(jnp.bfloat16)
    gate_set, up_set = (
        lax.all_gather(gate_delta, "gz", axis=0, tiled=True),
        lax.all_gather(up_delta, "gz", axis=0, tiled=True),
    )
    gate_cols, up_cols, hidden_cols = (
        lax.all_to_all(gate_set, "gy", split_axis=1, concat_axis=0, tiled=True),
        lax.all_to_all(up_set, "gy", split_axis=1, concat_axis=0, tiled=True),
        lax.all_to_all(hidden_set, "gy", split_axis=1, concat_axis=0, tiled=True),
    )
    first = lax.dot_general(gate_set, gate_full, back_dims, preferred_element_type=jnp.float32)
    input_grad = lax.psum_scatter(
        (
            first + lax.dot_general(up_set, up_full, back_dims, preferred_element_type=jnp.float32)
        ).astype(jnp.bfloat16),
        "gx",
        scatter_dimension=0,
        tiled=True,
    ).astype(jnp.float32)
    input_grad = input_grad.astype(jnp.bfloat16)
    row_dims = (((0,), (0,)), ((), ()))
    gate_grad = lax.dot_general(tok_all, gate_cols, row_dims, preferred_element_type=jnp.float32)
    up_grad = lax.dot_general(tok_all, up_cols, row_dims, preferred_element_type=jnp.float32)
    down_grad = lax.dot_general(hidden_cols, grad_all, row_dims, preferred_element_type=jnp.float32)
    gate_grad, up_grad, down_grad = (
        lax.psum(gate_grad.astype(jnp.bfloat16), "dp").astype(jnp.float32),
        lax.psum(up_grad.astype(jnp.bfloat16), "dp").astype(jnp.float32),
        lax.psum(down_grad.astype(jnp.bfloat16), "dp").astype(jnp.float32),
    )
    return (
        output,
        input_grad,
        gate_grad.astype(jnp.bfloat16),
        up_grad.astype(jnp.bfloat16),
        down_grad.astype(jnp.bfloat16),
    )


def solution(mesh):
    placed = (
        P(("dp", "gx", "gy"), "gz"),
        P("gz", ("gx", "gy")),
        P("gz", ("gx", "gy")),
        P(("gx", "gy"), "gz"),
        P(("dp", "gx", "gy"), "gz"),
    )
    return jax.shard_map(
        body,
        mesh=mesh,
        in_specs=placed,
        out_specs=(
            P(("dp", "gx", "gy"), "gz"),
            P(("dp", "gx", "gy"), "gz"),
            P("gz", ("gx", "gy")),
            P("gz", ("gx", "gy")),
            P(("gx", "gy"), "gz"),
        ),
        check_vma=False,
    )
```

profile of v0, /device:TPU:1, one launch (start us, length us, event | category | flops | bytes accessed | tf_op | source)
XLA Modules:
  0.0 449.4 jit_solution(2416971623413113218)
XLA Ops:
  9.4 20.8 %all_gather.35 = bf16[128,512]{1,0:T(8,128)(2,1)S(1)} all-gather(bf16[16,512]{1,0:T(8,128)(2,1)} %param.9), channel_id=1, replica_groups=mesh['dp'=2,'gx'=8,'gy'=4,'gz'=8] {'gx'}, dimensions={0}, use_global_device_ids=true | all-gather | bytes 147456 | tf_op jit(solution)/shard_map/all_gather | solution.py:10
  30.3 19.9 %all-gather.8.cloned.1.call-done = bf16[1856,512]{1,0:T(8,128)(2,1)} async-done(((bf16[464,512]{1,0:T(8,128)(2,1)}), bf16[1856,512]{1,0:T(8,128)(2,1)}) %all-gather.8.cloned.1.call-update) | async-done | bytes 1900560 | tf_op jit(solution)/shard_map/all_gather | solution.py:35
  50.2 3.1 convolution_convert_fusion
  53.3 19.9 %all_gather.30 = bf16[128,512]{1,0:T(8,128)(2,1)S(1)} all-gather(bf16[16,512]{1,0:T(8,128)(2,1)S(1)} %copy-done.5), channel_id=1, replica_groups=mesh['dp'=2,'gx'=8,'gy'=4,'gz'=8] {'gx'}, dimensions={0}, use_global_device_ids=true | all-gather | bytes 147456 | tf_op jit(solution)/shard_map/all_gather | solution.py:9
  73.2 13.7 %all-gather.4.cloned.1.call-done = bf16[512,1856]{0,1:T(8,128)(2,1)} async-done(((bf16[512,464]{0,1:T(8,128)(2,1)}), bf16[512,1856]{0,1:T(8,128)(2,1)}) %all-gather.4.cloned.1.call-update) | async-done | bytes 1900560 | tf_op jit(solution)/shard_map/all_gather | solution.py:18
  86.9 3.1 convolution_convert_fusion.2
  90.0 33.6 %all-gather.6.cloned.1.call-done = bf16[512,1856]{0,1:T(8,128)(2,1)} async-done(((bf16[512,464]{0,1:T(8,128)(2,1)}), bf16[512,1856]{0,1:T(8,128)(2,1)}) %all-gather.6.cloned.1.call-update) | async-done | bytes 1900560 | tf_op jit(solution)/shard_map/all_gather | solution.py:19
  123.6 3.1 convolution_convert_fusion.1
  126.7 10.6 %all_gather.38 = bf16[512,512]{1,0:T(8,128)(2,1)} all-gather(bf16[128,512]{1,0:T(8,128)(2,1)S(1)} %all_gather.30), channel_id=1, replica_groups=mesh['dp'=2,'gx'=8,'gy'=4,'gz'=8] {'gy'}, dimensions={0}, use_global_device_ids=true | all-gather | bytes 655360 | tf_op jit(solution)/shard_map/all_gather | solution.py:13
  137.4 10.8 %all_gather.39 = bf16[512,512]{1,0:T(8,128)(2,1)S(1)} all-gather(bf16[128,512]{1,0:T(8,128)(2,1)S(1)} %all_gather.35), channel_id=1, replica_groups=mesh['dp'=2,'gx'=8,'gy'=4,'gz'=8] {'gy'}, dimensions={0}, use_global_device_ids=true | all-gather | bytes 655360 | tf_op jit(solution)/shard_map/all_gather | solution.py:14
  148.1 17.3 %reduce-scatter.12.cloned.1.call-done = bf16[16,1856]{1,0:T(8,128)(2,1)} async-done(((bf16[128,1856]{1,0:T(8,128)(2,1)}), bf16[16,1856]{1,0:T(8,128)(2,1)}) %reduce-scatter.12.cloned.1.call-update) | async-done | bytes 59408 | tf_op jit(solution)/shard_map/reduce_scatter | solution.py:44
  165.5 41.3 %reduce-scatter.6.cloned.1.call-done = bf16[16,1856]{1,0:T(8,128)(2,1)} async-done(((bf16[128,1856]{1,0:T(8,128)(2,1)}), bf16[16,1856]{1,0:T(8,128)(2,1)}) %reduce-scatter.6.cloned.1.call-update) | async-done | bytes 59408 | tf_op jit(solution)/shard_map/reduce_scatter | solution.py:24
  206.8 41.0 %reduce-scatter.8.cloned.1.call-done = bf16[16,1856]{1,0:T(8,128)(2,1)} async-done(((bf16[128,1856]{1,0:T(8,128)(2,1)}), bf16[16,1856]{1,0:T(8,128)(2,1)}) %reduce-scatter.8.cloned.1.call-update) | async-done | bytes 59408 | tf_op jit(solution)/shard_map/reduce_scatter | solution.py:27
  248.8 17.3 %all_gather.33 = bf16[128,1856]{1,0:T(8,128)(2,1)S(1)} all-gather(bf16[16,1856]{1,0:T(8,128)(2,1)S(1)} %get-tuple-element.10), channel_id=1, replica_groups=mesh['dp'=2,'gx'=8,'gy'=4,'gz'=8] {'gz'}, dimensions={0}, use_global_device_ids=true | all-gather | bytes 534528 | tf_op jit(solution)/shard_map/all_gather | solution.py:34
  266.1 14.9 %all_gather.36 = bf16[128,1856]{1,0:T(8,128)(2,1)S(1)} all-gather(bf16[16,1856]{1,0:T(8,128)(2,1)S(1)} %get-tuple-element.9), channel_id=1, replica_groups=mesh['dp'=2,'gx'=8,'gy'=4,'gz'=8] {'gz'}, dimensions={0}, use_global_device_ids=true | all-gather | bytes 534528 | tf_op jit(solution)/shard_map/all_gather | solution.py:57
  282.0 5.2 %all-to-all-start = ((bf16[128,4,464]{0,2,1:T(8,128)(2,1)}), bf16[128,4,464]{0,2,1:T(8,128)(2,1)}, u32[]{:S(2)}, u32[]{:S(2)}) async-start(bf16[128,4,464]{0,2,1:T(8,128)(2,1)} %bitcast), calls=%async_computation.5 | async-start | bytes 950272 | tf_op jit(solution)/shard_map/all_to_all | solution.py:61
  288.1 1.1 convolution_convert_fusion.6
  289.2 15.6 %all_gather.37 = bf16[128,1856]{1,0:T(8,128)(2,1)S(1)} all-gather(bf16[16,1856]{1,0:T(8,128)(2,1)S(1)} %get-tuple-element.8), channel_id=1, replica_groups=mesh['dp'=2,'gx'=8,'gy'=4,'gz'=8] {'gz'}, dimensions={0}, use_global_device_ids=true | all-gather | bytes 534528 | tf_op jit(solution)/shard_map/all_gather | solution.py:58
  304.9 1.0 copy.12
  305.9 4.9 %all-to-all-start.1 = ((bf16[128,4,464]{0,2,1:T(8,128)(2,1)}), bf16[128,4,464]{0,2,1:T(8,128)(2,1)}, u32[]{:S(2)}, u32[]{:S(2)}) async-start(bf16[128,4,464]{0,2,1:T(8,128)(2,1)} %bitcast.3), calls=%async_computation.6 | async-start | bytes 950272 | tf_op jit(solution)/shard_map/all_to_all | solution.py:62
  311.3 1.1 copy-done.1
  312.3 1.1 fusion.2
  313.5 6.1 %all-to-all-done.1 = bf16[128,4,464]{0,2,1:T(8,128)(2,1)} async-done(((bf16[128,4,464]{0,2,1:T(8,128)(2,1)}), bf16[128,4,464]{0,2,1:T(8,128)(2,1)}, u32[]{:S(2)}, u32[]{:S(2)}) %all-to-all-start.1) | async-done | bytes 475168 | tf_op jit(solution)/shard_map/all_to_all | solution.py:62
  319.5 3.5 all-to-all-start.2
  323.1 2.2 fusion
  325.3 2.2 fusion.1
  327.5 2.9 all-to-all-done.2
  330.4 1.2 convolution_convert_fusion.3
  331.6 32.6 %reduce-scatter.14.cloned.1.call-done = bf16[16,512]{1,0:T(8,128)(2,1)} async-done(((bf16[128,512]{1,0:T(8,128)(2,1)}), bf16[16,512]{1,0:T(8,128)(2,1)}) %reduce-scatter.14.cloned.1.call-update) | async-done | bytes 16400 | tf_op jit(solution)/shard_map/reduce_scatter | solution.py:66
  364.2 74.2 %all-reduce.3.cloned.1.call-done = (bf16[512,464]{0,1:T(8,128)(2,1)}, bf16[512,464]{0,1:T(8,128)(2,1)}, bf16[464,512]{1,0:T(8,128)(2,1)}) async-done(((bf16[512,464]{0,1:T(8,128)(2,1)}, bf16[512,464]{0,1:T(8,128)(2,1)}, bf16[464,512]{1,0:T(8,128)(2,1)}), (bf16[512,464]{0,1:T(8,128)(2,1)}, bf16[512,464]{0,1:T(8,128)(2,1)}, bf16[464,512]{1,0:T(8,128)(2,1)})) %all-reduce.3.cloned.1.call-update) | async-done | bytes 1425424 | tf_op jit(solution)/shard_map/psum | solution.py:80
  438.4 1.9 copy.34
  440.3 1.8 copy.35
  (36 shorter events, 6.6 us)
Async XLA Ops:
  7.2 43.0 %all-gather.8.cloned.1.call-start = ((), (), s32[]{:S(2)}) async-start(), calls=%async_computation.12 | async-start | bytes 2375680 | tf_op jit(solution)/shard_map/all_gather | solution.py:35
  7.9 79.0 %all-gather.4.cloned.1.call-start = ((), (), s32[]{:S(2)}) async-start(), calls=%async_computation.8 | async-start | bytes 2375680 | tf_op jit(solution)/shard_map/all_gather | solution.py:18
  8.6 44.7 %copy-start.5 = (bf16[16,512]{1,0:T(8,128)(2,1)S(1)}, bf16[16,512]{1,0:T(8,128)(2,1)}, u32[]{:S(2)}) copy-start(bf16[16,512]{1,0:T(8,128)(2,1)} %param.5) | copy-start | bytes 49156
  8.7 114.9 %all-gather.6.cloned.1.call-start = ((), (), s32[]{:S(2)}) async-start(), calls=%async_computation.10 | async-start | bytes 2375680 | tf_op jit(solution)/shard_map/all_gather | solution.py:19
  9.4 156.1 %reduce-scatter.12.cloned.1.call-start = ((), (), s32[]{:S(2)}) async-start(), calls=%async_computation.14 | async-start | bytes 552960 | tf_op jit(solution)/shard_map/reduce_scatter | solution.py:44
  53.3 153.5 %reduce-scatter.6.cloned.1.call-start = ((), (), s32[]{:S(2)}) async-start(), calls=%async_computation.9 | async-start | bytes 552960 | tf_op jit(solution)/shard_map/reduce_scatter | solution.py:24
  90.0 157.8 %reduce-scatter.8.cloned.1.call-start = ((), (), s32[]{:S(2)}) async-start(), calls=%async_computation.11 | async-start | bytes 552960 | tf_op jit(solution)/shard_map/reduce_scatter | solution.py:27
  248.8 39.3 %copy-start.2 = (bf16[1856,512]{1,0:T(8,128)(2,1)S(1)}, bf16[1856,512]{1,0:T(8,128)(2,1)}, u32[]{:S(2)}) copy-start(bf16[1856,512]{1,0:T(8,128)(2,1)} %all-gather.8.cloned.1.call-done) | copy-start | bytes 5701636
  282.0 23.9 %all-to-all-start = ((bf16[128,4,464]{0,2,1:T(8,128)(2,1)}), bf16[128,4,464]{0,2,1:T(8,128)(2,1)}, u32[]{:S(2)}, u32[]{:S(2)}) async-start(bf16[128,4,464]{0,2,1:T(8,128)(2,1)} %bitcast), calls=%async_computation.5 | async-start | bytes 950272 | tf_op jit(solution)/shard_map/all_to_all | solution.py:61
  287.1 44.5 %reduce-scatter.10.cloned.1.call-start = ((), (), s32[]{:S(2)}) async-start(), calls=%async_computation.13 | async-start | bytes 147456 | tf_op jit(solution)/shard_map/reduce_scatter | solution.py:37
  289.2 21.6 %copy-start = (bf16[512,1856]{0,1:T(8,128)(2,1)S(1)}, bf16[512,1856]{0,1:T(8,128)(2,1)}, u32[]{:S(2)}) copy-start(bf16[512,1856]{0,1:T(8,128)(2,1)} %all-gather.4.cloned.1.call-done) | copy-start | bytes 5701636
  305.9 13.7 %all-to-all-start.1 = ((bf16[128,4,464]{0,2,1:T(8,128)(2,1)}), bf16[128,4,464]{0,2,1:T(8,128)(2,1)}, u32[]{:S(2)}, u32[]{:S(2)}) async-start(bf16[128,4,464]{0,2,1:T(8,128)(2,1)} %bitcast.3), calls=%async_computation.6 | async-start | bytes 950272 | tf_op jit(solution)/shard_map/all_to_all | solution.py:62
  310.8 53.4 %reduce-scatter.14.cloned.1.call-start = ((), (), s32[]{:S(2)}) async-start(), calls=%async_computation.15 | async-start | bytes 147456 | tf_op jit(solution)/shard_map/reduce_scatter | solution.py:66
  310.8 1.5 copy-start.1
  312.3 10.7 %copy-start.3 = (bf16[512,512]{1,0:T(8,128)(2,1)S(1)}, bf16[512,512]{1,0:T(8,128)(2,1)}, u32[]{:S(2)}) copy-start(bf16[512,512]{1,0:T(8,128)(2,1)} %all_gather.38) | copy-start | bytes 1572868
  319.5 10.8 %all-to-all-start.2 = ((bf16[128,4,464]{0,2,1:T(8,128)(2,1)}), bf16[128,4,464]{0,2,1:T(8,128)(2,1)S(1)}, u32[]{:S(2)}, u32[]{:S(2)}) async-start(bf16[128,4,464]{0,2,1:T(8,128)(2,1)} %bitcast.6), calls=%async_computation.7 | async-start | bytes 950272 | tf_op jit(solution)/shard_map/all_to_all | solution.py:63
  323.0 115.4 %all-reduce.3.cloned.1.call-start = ((), (), s32[]{:S(2)}) async-start(), calls=%async_computation.16 | async-start | bytes 2850816 | tf_op jit(solution)/shard_map/psum | solution.py:80
  438.4 3.7 copy-start.4
Sparse Core Ops, SparseCore 0:
  10.1 40.0 all-gather.7
  52.3 34.5 all-gather.3
  89.0 34.5 all-gather.5
  126.3 39.1 reduce-scatter.11
  168.3 38.4 reduce-scatter.5
  209.5 38.3 reduce-scatter.7
  291.5 31.9 reduce-scatter.9
  326.9 37.2 reduce-scatter.13
  368.2 70.1 all-reduce.2
where the time goes:
time: 450 us; the launch traced here: 449 us
  waiting for transfers between devices  285 us (63%)
  blocking collectives  110 us (24%)
  matrix products  17.5 us (4%)
  starting transfers between devices  13.9 us (3%)
  between operations  13.9 us (3%)
  local copies, waits for them, and re-layouts  8.53 us (2%)
    psum x1, waiting for transfers between devices, body(): lax.psum(gate_grad.astype(jnp.bfloat16), 'dp').astype(jnp.float32)  74.2 us
    reduce_scatter x1, waiting for transfers between devices, body(): lax.psum_scatter(gate_part.astype(jnp.bfloat16), 'gz', scatter_dimension=...  41.3 us
    reduce_scatter x1, waiting for transfers between devices, body(): lax.psum_scatter(up_part.astype(jnp.bfloat16), 'gz', scatter_dimension=0,...  41 us
    all_gather x1, waiting for transfers between devices, body(): lax.all_gather(up_weight, 'gy', axis=1, tiled=True)  33.6 us
    reduce_scatter x1, waiting for transfers between devices, body(): lax.psum_scatter((first + lax.dot_general(up_set, up_full, back_dims, pre...  32.6 us
    all_gather x1, blocking collectives, body(): lax.all_gather(out_grad, 'gx', axis=0, tiled=True)  20.8 us
    all_gather x1, waiting for transfers between devices, body(): down_full = lax.all_gather(down_weight, 'gy', axis=0, tiled=True)  19.9 us
    all_gather x1, blocking collectives, body(): lax.all_gather(tokens, 'gx', axis=0, tiled=True)  19.9 us
  transfers between devices with their start and end apart: 12, of which 10 were waited for; matrix products, arithmetic and copies ran while one was open for 4% of the time, Pallas kernels for 0%

commit v1 on v0

v1 whole, which is shorter than its diff:
```python
import jax
import jax.numpy as jnp
from jax import lax
from jax.experimental import pallas as pl
from jax.experimental.pallas import tpu as pltpu
from jax.sharding import PartitionSpec as P

BF = jnp.bfloat16
F32 = jnp.float32
HALF = 240
LAST = 224
NT = (((1,), (1,)), ((), ()))
TN = (((0,), (0,)), ((), ()))
NN = (((1,), (0,)), ((), ()))
FAR = (4, 3, 5, 2, 6, 1, 7)


def kernel(
    tok_ref, grad_ref, wg_ref, wu_ref, wd_ref,
    out_ref, ing_ref, gg_ref, ug_ref, dg_ref,
    T, W, PM, SC, RC, SZ, RZ, V, D, OB, RX, SY, RY, WG, FO,
    lsem, ssem, rsem,
):
    dp, gx, gy, gz = (lax.axis_index(a) for a in ("dp", "gx", "gy", "gz"))
    zh, c = lax.div(gz, 2), lax.rem(gz, 2)
    other = 1 - c
    odp = 1 - dp

    def ydev(k):
        return (dp, lax.rem(gx + k, 8), gy, gz)

    def xdev(k):
        return (dp, gx, lax.rem(gy + k, 4), gz)

    def zdev(k):
        return (dp, gx, gy, lax.rem(zh + k, 4) * 2 + c)

    core = (dp, gx, gy, zh * 2 + other)
    near_a = (odp, gx, gy, gz)
    near_b = (odp, gx, gy, lax.rem(zh + 3 + 2 * dp, 4) * 2 + c)

    count = [0]
    sent = []

    def send(src, dst, device):
        i = count[0]
        count[0] += 1
        copy = pltpu.make_async_remote_copy(
            src_ref=src,
            dst_ref=dst,
            send_sem=ssem.at[i],
            recv_sem=rsem.at[i],
            device_id=device,
            device_id_type=pl.DeviceIdType.MESH,
        )
        copy.start()
        sent.append(copy)
        return copy

    def arrive(copies):
        for copy in copies:
            copy.wait_recv()

    lcount = [0]

    def local(src, dst):
        i = lcount[0]
        lcount[0] += 1
        copy = pltpu.make_async_copy(src, dst, lsem.at[i])
        copy.start()
        return copy

    tok_in = [local(tok_ref, T.at[0, dp, gx, gy]), local(grad_ref, T.at[1, dp, gx, gy])]
    w_in = []
    for q, ref in enumerate((wg_ref, wu_ref, wd_ref)):
        w_in.append(local(ref.at[pl.ds(0, HALF)], W.at[q, 0]))
        w_in.append(local(ref.at[pl.ds(HALF, LAST)], W.at[q, 1, pl.ds(0, LAST)]))

    barrier = pltpu.get_barrier_semaphore()
    partners = [ydev(k) for k in FAR] + [xdev(k) for k in (2, 1, 3)] + [zdev(k) for k in (2, 1, 3)]
    partners += [near_a, near_b, core]
    for device in partners:
        pl.semaphore_signal(barrier, inc=1, device_id=device, device_id_type=pl.DeviceIdType.MESH)
    for q in range(3):
        W[q, 1, LAST:, :] = jnp.zeros((HALF - LAST, 512), BF)
    for copy in tok_in:
        copy.wait()
    pl.semaphore_wait(barrier, len(partners))

    def ysends(a, d, whole):
        ref = T.at[a, d, gx] if whole else T.at[a, d, gx, gy]
        return [send(ref, ref, ydev(k)) for k in FAR]

    def xsends(a, d, whole):
        ref = T.at[a, d, :, gy] if whole else T.at[a, d, gx, gy]
        return [send(ref, ref, xdev(k)) for k in (2, 1, 3)]

    tok_y = ysends(0, dp, False)
    grad_x = xsends(1, dp, False)
    swap = [send(T.at[a, dp, gx, gy], T.at[a, dp, gx, gy], near_a) for a in range(2)]
    arrive(tok_y)
    tok_x = xsends(0, dp, True)
    arrive(grad_x)
    grad_y = ysends(1, dp, True)
    for copy in w_in:
        copy.wait()
    arrive(tok_x)

    def project(q, x):
        far = lax.dot_general(W[q, other], x, NT, preferred_element_type=F32)
        for j in range(4):
            SC[q, j] = far[:, 128 * j : 128 * j + 128].astype(BF)
        copy = send(SC.at[q], RC.at[q], core)
        mine = lax.dot_general(W[q, c], x, NT, preferred_element_type=F32)
        for j in range(4):
            PM[q, j] = mine[:, 128 * j : 128 * j + 128]
        return copy

    def scatter(q, copy):
        copy.wait_recv()
        copies = []
        for k in (2, 1, 3):
            j = lax.rem(zh + k, 4)
            SZ[q, k - 1] = (PM[q, j] + RC[q, j].astype(F32)).astype(BF)
            copies.append(send(SZ.at[q, k - 1], RZ.at[q, k - 1], zdev(k)))
        return copies

    def total(q, copies):
        arrive(copies)
        value = PM[q, zh] + RC[q, zh].astype(F32)
        for k in range(3):
            value = value + RZ[q, k].astype(F32)
        return value

    x = T[0, dp].reshape(512, 512)
    gate_c = project(0, x)
    up_c = project(1, x)
    gate_z = scatter(0, gate_c)
    up_z = scatter(1, up_c)
    arrive(swap)
    other_y = ysends(0, odp, False)
    other_x = xsends(1, odp, False)
    arrive(grad_y)
    hg_c = project(2, T[1, dp].reshape(512, 512))
    hg_z = scatter(2, hg_c)
    arrive(other_y)
    other_y = xsends(0, odp, True)
    arrive(other_x)
    other_x = ysends(1, odp, True)

    def spread(q, value):
        D[q, dp, c, zh] = value.astype(BF)
        ref = D.at[q, dp, c, zh]
        return [send(ref, ref, zdev(k)) for k in (2, 1, 3)], [send(ref, ref, core)]

    gate_val = total(0, gate_z)
    up_val = total(1, up_z)
    gate_sig = jax.nn.sigmoid(gate_val)
    gate_act = gate_val * gate_sig
    V[0] = up_val * gate_sig * (1.0 + gate_val * (1.0 - gate_sig))
    V[1] = gate_act
    h_z, h_c = spread(0, gate_act * up_val)
    hid_grad = total(2, hg_z)
    gd_z, gd_c = spread(1, hid_grad * V[0])
    ud_z, ud_c = spread(2, hid_grad * V[1])

    def forward(q, copies, to_core):
        for k, copy in zip((2, 1, 3), copies, strict=True):
            copy.wait_recv()
            ref = D.at[q, dp, c, lax.rem(zh + 4 - k, 4)]
            to_core.append(send(ref, ref, core))

    def swap_dp(q):
        low, high = D.at[q, dp, c, pl.ds(0, 2)], D.at[q, dp, c, pl.ds(2, 2)]
        return [send(low, low, near_a), send(high, high, near_b)]

    def rows(q, d):
        halves = [
            jnp.concatenate([D[q, d, h, j] for j in range(4)], axis=1) for h in range(2)
        ]
        return jnp.concatenate(halves, axis=0)

    def x_scatter(o, part):
        OB[o] = part.astype(BF).reshape(8, 4, 16, 512)
        return [
            send(OB.at[o, :, lax.rem(gy + k, 4)], RX.at[o, k - 1], xdev(k)) for k in (2, 1, 3)
        ]

    def y_scatter(o, copies):
        arrive(copies)
        value = OB[o, :, gy].astype(F32)
        for k in range(3):
            value = value + RX[o, k].astype(F32)
        SY[o] = value.astype(BF)
        return [send(SY.at[o, lax.rem(gx + k, 8)], RY.at[o, k - 1], ydev(k)) for k in FAR]

    def finish(o, copies, ref):
        arrive(copies)
        value = SY[o, gx].astype(F32)
        for k in range(7):
            value = value + RY[o, k].astype(F32)
        FO[o] = value.astype(BF)
        return local(FO.at[o], ref)

    forward(0, h_z, h_c)
    arrive(h_c)
    out_x = x_scatter(0, lax.dot_general(rows(0, dp), W[2].reshape(480, 512), TN, preferred_element_type=F32))
    forward(1, gd_z, gd_c)
    forward(2, ud_z, ud_c)
    deltas = [swap_dp(q) for q in range(3)]
    arrive(gd_c)
    arrive(ud_c)
    back = jnp.concatenate([rows(1, dp), rows(2, dp)], axis=0)
    in_x = x_scatter(1, lax.dot_general(back, W[0:2].reshape(960, 512), TN, preferred_element_type=F32))
    out_y = y_scatter(0, out_x)
    in_y = y_scatter(1, in_x)

    fwd = []
    for q in range(3):
        arrive(deltas[q])
        fwd.append(send(D.at[q, odp, c], D.at[q, odp, c], core))
    arrive(other_y)
    arrive(other_x)
    done = []
    for q, ref in ((0, dg_ref), (1, gg_ref), (2, ug_ref)):
        arrive([fwd[q]])
        right = T[1 if q == 0 else 0].reshape(1024, 512)
        for h in range(2):
            left = jnp.concatenate([D[q, d, h, j] for d in range(2) for j in range(4)], axis=1)
            value = lax.dot_general(left, right, NN, preferred_element_type=F32).astype(BF)
            if h == 0:
                WG[q, 0:HALF] = value
            else:
                WG[q, HALF : HALF + LAST] = value[0:LAST]
        done.append(local(WG.at[q], ref))
    done.append(finish(0, out_y, out_ref))
    done.append(finish(1, in_y, ing_ref))
    for copy in sent:
        copy.wait_send()
    for copy in done:
        copy.wait()


def body(tokens, gate_weight, up_weight, down_weight, out_grad):
    any_spec = pl.BlockSpec(memory_space=pl.ANY)
    small = jax.ShapeDtypeStruct((16, 512), BF)
    large = jax.ShapeDtypeStruct((464, 512), BF)
    output, input_grad, gate_t, up_t, down_grad = pl.pallas_call(
        kernel,
        out_shape=(small, small, large, large, large),
        in_specs=[any_spec] * 5,
        out_specs=(any_spec,) * 5,
        scratch_shapes=[
            pltpu.VMEM((2, 2, 8, 4, 16, 512), BF),
            pltpu.VMEM((3, 2, HALF, 512), BF),
            pltpu.VMEM((3, 4, HALF, 128), F32),
            pltpu.VMEM((3, 4, HALF, 128), BF),
            pltpu.VMEM((3, 4, HALF, 128), BF),
            pltpu.VMEM((3, 3, HALF, 128), BF),
            pltpu.VMEM((3, 3, HALF, 128), BF),
            pltpu.VMEM((2, HALF, 128), F32),
            pltpu.VMEM((3, 2, 2, 4, HALF, 128), BF),
            pltpu.VMEM((2, 8, 4, 16, 512), BF),
            pltpu.VMEM((2, 3, 8, 16, 512), BF),
            pltpu.VMEM((2, 8, 16, 512), BF),
            pltpu.VMEM((2, 7, 16, 512), BF),
            pltpu.VMEM((3, 464, 512), BF),
            pltpu.VMEM((2, 16, 512), BF),
            pltpu.SemaphoreType.DMA((16,)),
            pltpu.SemaphoreType.DMA((128,)),
            pltpu.SemaphoreType.DMA((128,)),
        ],
        compiler_params=pltpu.CompilerParams(
            collective_id=0, has_side_effects=True, vmem_limit_bytes=48 * 2**20
        ),
        name="block",
    )(tokens, out_grad, gate_weight.T, up_weight.T, down_weight)
    return output, input_grad, gate_t.T, up_t.T, down_grad


def solution(mesh):
    placed = (
        P(("dp", "gx", "gy"), "gz"),
        P("gz", ("gx", "gy")),
        P("gz", ("gx", "gy")),
        P(("gx", "gy"), "gz"),
        P(("dp", "gx", "gy"), "gz"),
    )
    return jax.shard_map(
        body,
        mesh=mesh,
        in_specs=placed,
        out_specs=(
            P(("dp", "gx", "gy"), "gz"),
            P(("dp", "gx", "gy"), "gz"),
            P("gz", ("gx", "gy")),
            P("gz", ("gx", "gy")),
            P(("gx", "gy"), "gz"),
        ),
        check_vma=False,
    )
```

time: 450 us -> 92.1 us (0.20)
  waiting for transfers between devices: 285 us -> 0 us
  blocking collectives: 110 us -> 0 us
  Pallas kernels: 0 us -> 83 us
  matrix products: 17.5 us -> 0 us
  starting transfers between devices: 13.9 us -> 0 us
  between operations: 13.9 us -> 0.66 us
    reduce_scatter x5 -> x0, waiting for transfers between devices: 132 us -> none  [the longest x1 41.3 us: body(): lax.psum_scatter(gate_part.astype(jnp.bfloat16), 'gz', scatter_dimension=...]
    all_gather x7 -> x0, blocking collectives: 110 us -> none  [the longest x1 20.8 us: body(): lax.all_gather(out_grad, 'gx', axis=0, tiled=True)]
    pallas_call x0 -> x1, Pallas kernels: none -> 83 us  [body(): pl.pallas_call(kernel, out_shape=(small, small, large, large, large), in_...]
    psum x1 -> x0, waiting for transfers between devices: 74.2 us -> none  [body(): lax.psum(gate_grad.astype(jnp.bfloat16), 'dp').astype(jnp.float32)]
    all_gather x3 -> x0, waiting for transfers between devices: 67.1 us -> none  [the longest x1 33.6 us: body(): lax.all_gather(up_weight, 'gy', axis=1, tiled=True)]
    dot_general x9 -> x0, matrix products: 17.5 us -> none  [the longest x1 3.09 us: body(): gate_part = jnp.dot(tok_set, gate_full, preferred_element_type=jnp.float32)]
    all_to_all x3 -> x0, starting transfers between devices: 13.6 us -> none  [the longest x1 5.17 us: body(): lax.all_to_all(gate_set, 'gy', split_axis=1, concat_axis=0, tiled=True)]
    all_to_all x3 -> x0, waiting for transfers between devices: 8.96 us -> none  [the longest x1 6.07 us: body(): lax.all_to_all(up_set, 'gy', split_axis=1, concat_axis=0, tiled=True)]
  transfers between devices with their start and end apart: 12 -> 0, of which waited for: 10 -> 0; matrix products, arithmetic and copies ran while one was open for 4% -> 0% of each run, Pallas kernels for 0% -> 0%
where the time goes in v1:
time: 92.1 us; the launch traced here: 91.7 us
  Pallas kernels  83 us (90%)
  local copies, waits for them, and re-layouts  8.03 us (9%)
    pallas_call x1, Pallas kernels, body(): pl.pallas_call(kernel, out_shape=(small, small, large, large, large), in_...  83 us
    unnamed x15, local copies, waits for them, and re-layouts  8.03 us

profile of v1, /device:TPU:1, one launch (start us, length us, event | category | flops | bytes accessed | tf_op | source)
XLA Modules:
  0.0 91.7 jit_solution(18173520244777661542)
XLA Ops:
  0.6 0.0 copy-start
  0.6 1.0 %copy-done = bf16[512,464]{0,1:T(8,128)(2,1)S(1)} copy-done((bf16[512,464]{0,1:T(8,128)(2,1)S(1)}, bf16[512,464]{0,1:T(8,128)(2,1)}, u32[]{:S(2)}) %copy-start) | copy-done | bytes 475160
  1.7 0.0 copy-start.1
  1.7 1.0 %copy-done.1 = bf16[512,464]{0,1:T(8,128)(2,1)S(1)} copy-done((bf16[512,464]{0,1:T(8,128)(2,1)S(1)}, bf16[512,464]{0,1:T(8,128)(2,1)}, u32[]{:S(2)}) %copy-start.1) | copy-done | bytes 475160
  2.7 0.0 copy-start.2
  2.7 1.0 %copy-done.2 = bf16[464,512]{1,0:T(8,128)(2,1)S(1)} copy-done((bf16[464,512]{1,0:T(8,128)(2,1)S(1)}, bf16[464,512]{1,0:T(8,128)(2,1)}, u32[]{:S(2)}) %copy-start.2) | copy-done | bytes 475160
  3.7 0.0 copy-start.3
  3.7 0.7 copy-done.3
  4.4 0.0 copy-start.4
  4.4 0.7 copy-done.4
  5.1 83.0 %block.1 = (bf16[16,512]{1,0:T(8,128)(2,1)S(1)}, bf16[16,512]{1,0:T(8,128)(2,1)S(1)}, bf16[464,512]{1,0:T(8,128)(2,1)S(1)}, bf16[464,512]{1,0:T(8,128)(2,1)S(1)}, bf16[464,512]{1,0:T(8,128)(2,1)S(1)}) custom-call(bf16[16,512]{1,0:T(8,128)(2,1)S(1)} %copy-done.3, bf16[16,512]{1,0:T(8,128)(2,1)S(1)} %copy-done.4, bf16[464,512]{1,0:T(8,128)(2,1)S(1)} %bitcast.4, ...), custom_call_target="tpu_custom_call" | custom-call | tf_op jit(solution)/shard_map/block/pallas_call | solution.py:248
  88.2 0.6 copy.15
  88.8 0.6 copy.16
  89.4 0.8 copy.17
  90.1 0.8 copy.18
  90.9 0.8 copy.19
Async XLA Ops:
  0.6 1.0 %copy-start = (bf16[512,464]{0,1:T(8,128)(2,1)S(1)}, bf16[512,464]{0,1:T(8,128)(2,1)}, u32[]{:S(2)}) copy-start(bf16[512,464]{0,1:T(8,128)(2,1)} %param.6) | copy-start | bytes 1425412
  1.7 1.0 %copy-start.1 = (bf16[512,464]{0,1:T(8,128)(2,1)S(1)}, bf16[512,464]{0,1:T(8,128)(2,1)}, u32[]{:S(2)}) copy-start(bf16[512,464]{0,1:T(8,128)(2,1)} %param.7) | copy-start | bytes 1425412
  2.7 1.0 %copy-start.2 = (bf16[464,512]{1,0:T(8,128)(2,1)S(1)}, bf16[464,512]{1,0:T(8,128)(2,1)}, u32[]{:S(2)}) copy-start(bf16[464,512]{1,0:T(8,128)(2,1)} %wd_ref.1) | copy-start | bytes 1425412
  3.7 0.7 copy-start.3
  4.4 0.7 copy-start.4

commit v2 on v1

v2 whole, which is shorter than its diff:
```python
import jax
import jax.numpy as jnp
from jax import lax
from jax.experimental import pallas as pl
from jax.experimental.pallas import tpu as pltpu
from jax.sharding import PartitionSpec as P

BF = jnp.bfloat16
F32 = jnp.float32
HALF = 240
LAST = 224
CUT = 128
NT = (((1,), (1,)), ((), ()))
TN = (((0,), (0,)), ((), ()))
NN = (((1,), (0,)), ((), ()))
FAR = (4, 3, 5, 2, 6, 1, 7)


def kernel(
    tok_ref, grad_ref, wg_ref, wu_ref, wd_ref,
    out_ref, ing_ref, gg_ref, ug_ref, dg_ref,
    T, W, PM, SC, RC, SZ, RA, RZ, V, D, OB, RX, SY, RY, WG, FO,
    lsem, ssem, rsem,
):
    dp, gx, gy, gz = (lax.axis_index(a) for a in ("dp", "gx", "gy", "gz"))
    zh, c = lax.div(gz, 2), lax.rem(gz, 2)
    z = 2 * zh + dp
    other = 1 - c
    odp = 1 - dp

    def ydev(k):
        return (dp, lax.rem(gx + k, 8), gy, gz)

    def xdev(k):
        return (dp, gx, lax.rem(gy + k, 4), gz)

    def zdev(k):
        there = lax.rem(z + k + 8, 8)
        return (lax.rem(there, 2), gx, gy, lax.div(there, 2) * 2 + c)

    core = (dp, gx, gy, zh * 2 + other)
    partner = (odp, gx, gy, gz)

    count = [0]
    sent = []

    def send(src, dst, device):
        i = count[0]
        count[0] += 1
        copy = pltpu.make_async_remote_copy(
            src_ref=src,
            dst_ref=dst,
            send_sem=ssem.at[i],
            recv_sem=rsem.at[i],
            device_id=device,
            device_id_type=pl.DeviceIdType.MESH,
        )
        copy.start()
        sent.append(copy)
        return copy

    def arrive(copies):
        for copy in copies:
            copy.wait_recv()

    lcount = [0]

    def local(src, dst):
        i = lcount[0]
        lcount[0] += 1
        copy = pltpu.make_async_copy(src, dst, lsem.at[i])
        copy.start()
        return copy

    tok_in = [local(tok_ref, T.at[0, dp, gx, gy]), local(grad_ref, T.at[1, dp, gx, gy])]
    w_in = []
    for q, ref in enumerate((wg_ref, wu_ref, wd_ref)):
        w_in.append(local(ref.at[pl.ds(0, HALF)], W.at[q, 0]))
        w_in.append(local(ref.at[pl.ds(HALF, LAST)], W.at[q, 1, pl.ds(0, LAST)]))

    barrier = pltpu.get_barrier_semaphore()
    partners = [ydev(k) for k in FAR] + [xdev(k) for k in (2, 1, 3)]
    partners += [zdev(k) for k in (2, -2, 1, -1)] + [core]
    for device in partners:
        pl.semaphore_signal(barrier, inc=1, device_id=device, device_id_type=pl.DeviceIdType.MESH)
    for q in range(3):
        W[q, 1, LAST:, :] = jnp.zeros((HALF - LAST, 512), BF)
    for copy in tok_in:
        copy.wait()
    pl.semaphore_wait(barrier, len(partners))

    def ysends(a, d, whole):
        ref = T.at[a, d, gx] if whole else T.at[a, d, gx, gy]
        return {k: send(ref, ref, ydev(k)) for k in FAR}

    def xsends(ref):
        return [send(ref, ref, xdev(k)) for k in (2, 1, 3)]

    tok_y = ysends(0, dp, False)
    tok_x = xsends(T.at[0, dp, gx, gy])
    grad_x = xsends(T.at[1, dp, gx, gy])
    swap = [send(T.at[a, dp, gx, gy], T.at[a, dp, gx, gy], partner) for a in range(2)]
    for copy in w_in:
        copy.wait()
    for k in (1, 7, 2, 6, 3, 5, 4):
        tok_y[k].wait_recv()
        tok_x += xsends(T.at[0, dp, lax.rem(gx + 8 - k, 8), gy])
        if k == 7:
            arrive(grad_x)
            grad_y = ysends(1, dp, True)
    arrive(tok_x)

    def project(q, x):
        far = lax.dot_general(W[q, other], x, NT, preferred_element_type=F32)
        for j in range(4):
            SC[q, j] = far[:, 128 * j : 128 * j + 128].astype(BF)
        copy = send(SC.at[q], RC.at[q], core)
        mine = lax.dot_general(W[q, c], x, NT, preferred_element_type=F32)
        for j in range(4):
            PM[q, j] = mine[:, 128 * j : 128 * j + 128]
        return copy

    def chunk(q, k):
        j = lax.rem(zh + k, 4)
        return PM[q, j] + RC[q, j].astype(F32)

    low, high = pl.ds(0, CUT), pl.ds(CUT, HALF - CUT)

    def scatter(q, copy):
        copy.wait_recv()
        SZ[q, 1] = chunk(q, 2).astype(BF)
        first = [
            send(SZ.at[q, 1, low], RA.at[q, low], zdev(2)),
            send(SZ.at[q, 1, high], RA.at[q, high], zdev(-2)),
        ]
        SZ[q, 0, CUT:] = chunk(q, 1)[CUT:].astype(BF)
        SZ[q, 2, :CUT] = chunk(q, 3)[:CUT].astype(BF)
        second = [
            send(SZ.at[q, 0, high], RZ.at[q, 0, high], zdev(2)),
            send(SZ.at[q, 2, low], RZ.at[q, 1, low], zdev(-2)),
        ]
        return first, second

    def relay(q, copies):
        first, second = copies
        first[0].wait_recv()
        SZ[q, 0, :CUT] = (chunk(q, 1)[:CUT] + RA[q, :CUT].astype(F32)).astype(BF)
        second.append(send(SZ.at[q, 0, low], RZ.at[q, 0, low], zdev(2)))
        first[1].wait_recv()
        SZ[q, 2, CUT:] = (chunk(q, 3)[CUT:] + RA[q, CUT:].astype(F32)).astype(BF)
        second.append(send(SZ.at[q, 2, high], RZ.at[q, 1, high], zdev(-2)))

    def total(q, copies):
        arrive(copies[1])
        return chunk(q, 0) + RZ[q, 0].astype(F32) + RZ[q, 1].astype(F32)

    x = T[0, dp].reshape(512, 512)
    gate_c = project(0, x)
    up_c = project(1, x)
    gate_z = scatter(0, gate_c)
    up_z = scatter(1, up_c)
    arrive(swap)
    other_y = ysends(0, odp, False)
    other_x = xsends(T.at[1, odp, gx, gy])
    relay(0, gate_z)
    relay(1, up_z)
    arrive(grad_y.values())
    hg_c = project(2, T[1, dp].reshape(512, 512))
    hg_z = scatter(2, hg_c)
    arrive(other_x)
    other_x = list(ysends(1, odp, True).values())
    arrive(other_y.values())
    other_y = xsends(T.at[0, odp, :, gy])
    relay(2, hg_z)

    right, left, to_core = {}, {}, {}

    def spread(q, value):
        D[q, c, z] = value.astype(BF)
        ref = D.at[q, c, z]
        right[q] = send(ref, ref, zdev(1))
        left[q] = send(ref, ref, zdev(-1))
        to_core[q] = [send(ref, ref, core)]

    def step(q, s):
        there, back = lax.rem(z + 8 - s, 8), lax.rem(z + s, 8)
        a, b = D.at[q, c, there], D.at[q, c, back]
        right[q].wait_recv()
        if s < 4:
            a_next = a if s < 3 else D.at[q, c, there, low]
            right[q] = send(a_next, a_next, zdev(1))
            to_core[q].append(send(a, a, core))
        left[q].wait_recv()
        if s < 4:
            b_next = b if s < 3 else D.at[q, c, back, high]
            left[q] = send(b_next, b_next, zdev(-1))
        to_core[q].append(send(b, b, core))

    def rows(q, d):
        halves = [
            jnp.concatenate([D[q, h, 2 * j + d] for j in range(4)], axis=1) for h in range(2)
        ]
        return jnp.concatenate(halves, axis=0)

    def x_scatter(o, part):
        part = part.astype(BF).reshape(8, 4, 16, 512)
        for g in range(8):
            OB[o, lax.rem(g + 14 - gx, 8)] = part[g]
        groups = []
        for h in range(2):
            block = pl.ds(4 * h, 4)
            groups.append([
                send(OB.at[o, block, lax.rem(gy + k, 4)], RX.at[o, k - 1, block], xdev(k))
                for k in (2, 1, 3)
            ])
        return groups

    def y_scatter(o, h, copies):
        arrive(copies[h])
        block = slice(4 * h, 4 * h + 4)
        value = OB[o, block, gy].astype(F32)
        for k in range(3):
            value = value + RX[o, k, block].astype(F32)
        SY[o, block] = value.astype(BF)
        order = (2, 1, 3, 0) if h == 0 else (4, 5, 7)
        return [send(SY.at[o, i], RY.at[o, (i + 2) % 8 - 1], ydev((i + 2) % 8)) for i in order]

    def finish(o, copies, ref):
        arrive(copies)
        value = SY[o, 6].astype(F32)
        for k in range(7):
            value = value + RY[o, k].astype(F32)
        FO[o] = value.astype(BF)
        return local(FO.at[o], ref)

    gate_val = total(0, gate_z)
    up_val = total(1, up_z)
    gate_sig = jax.nn.sigmoid(gate_val)
    gate_act = gate_val * gate_sig
    V[0] = up_val * gate_sig * (1.0 + gate_val * (1.0 - gate_sig))
    V[1] = gate_act
    spread(0, gate_act * up_val)
    step(0, 1)
    hid_grad = total(2, hg_z)
    spread(1, hid_grad * V[0])
    spread(2, hid_grad * V[1])
    step(0, 2)
    step(1, 1)
    step(2, 1)
    step(0, 3)
    step(1, 2)
    step(2, 2)
    step(0, 4)
    step(1, 3)
    step(2, 3)
    arrive(to_core[0])
    part = lax.dot_general(rows(0, dp), W[2].reshape(480, 512), TN, preferred_element_type=F32)
    out_x = x_scatter(0, part)
    step(1, 4)
    step(2, 4)
    arrive(to_core[1])
    arrive(to_core[2])
    both = jnp.concatenate([rows(1, dp), rows(2, dp)], axis=0)
    part = lax.dot_general(both, W[0:2].reshape(960, 512), TN, preferred_element_type=F32)
    in_x = x_scatter(1, part)
    out_y = y_scatter(0, 0, out_x) + y_scatter(0, 1, out_x)

    done = []

    def weight_grad(q, ref):
        right = T[1 if q == 0 else 0].reshape(1024, 512)
        for h in range(2):
            left = jnp.concatenate([D[q, h, 2 * j + d] for d in range(2) for j in range(4)], axis=1)
            value = lax.dot_general(left, right, NN, preferred_element_type=F32).astype(BF)
            if h == 0:
                WG[q, 0:HALF] = value
            else:
                WG[q, HALF : HALF + LAST] = value[0:LAST]
        done.append(local(WG.at[q], ref))

    arrive(other_y)
    arrive(other_x)
    weight_grad(0, dg_ref)
    in_y = y_scatter(1, 0, in_x)
    in_y += y_scatter(1, 1, in_x)
    weight_grad(1, gg_ref)
    weight_grad(2, ug_ref)
    done.append(finish(0, out_y, out_ref))
    done.append(finish(1, in_y, ing_ref))
    for copy in sent:
        copy.wait_send()
    for copy in done:
        copy.wait()


def store(*refs):
    n = (len(refs) - 1) // 3
    held, sem = refs[2 * n : 3 * n], refs[-1]
    fetch = [pltpu.make_async_copy(refs[i], held[i], sem.at[i]) for i in range(n)]
    put = [pltpu.make_async_copy(held[i], refs[n + i], sem.at[n + i]) for i in range(n)]
    for copy in fetch:
        copy.start()
    for i in range(n):
        fetch[i].wait()
        put[i].start()
    for copy in put:
        copy.wait()


def body(tokens, gate_weight, up_weight, down_weight, out_grad):
    any_spec = pl.BlockSpec(memory_space=pl.ANY)
    hbm_spec = pl.BlockSpec(memory_space=pltpu.HBM)
    small = jax.ShapeDtypeStruct((16, 512), BF)
    large = jax.ShapeDtypeStruct((464, 512), BF)
    results = pl.pallas_call(
        kernel,
        out_shape=(small, small, large, large, large),
        in_specs=[hbm_spec] * 5,
        out_specs=(any_spec,) * 5,
        scratch_shapes=[
            pltpu.VMEM((2, 2, 8, 4, 16, 512), BF),
            pltpu.VMEM((3, 2, HALF, 512), BF),
            pltpu.VMEM((3, 4, HALF, 128), F32),
            pltpu.VMEM((3, 4, HALF, 128), BF),
            pltpu.VMEM((3, 4, HALF, 128), BF),
            pltpu.VMEM((3, 3, HALF, 128), BF),
            pltpu.VMEM((3, HALF, 128), BF),
            pltpu.VMEM((3, 2, HALF, 128), BF),
            pltpu.VMEM((2, HALF, 128), F32),
            pltpu.VMEM((3, 2, 8, HALF, 128), BF),
            pltpu.VMEM((2, 8, 4, 16, 512), BF),
            pltpu.VMEM((2, 3, 8, 16, 512), BF),
            pltpu.VMEM((2, 8, 16, 512), BF),
            pltpu.VMEM((2, 7, 16, 512), BF),
            pltpu.VMEM((3, 464, 512), BF),
            pltpu.VMEM((2, 16, 512), BF),
            pltpu.SemaphoreType.DMA((16,)),
            pltpu.SemaphoreType.DMA((176,)),
            pltpu.SemaphoreType.DMA((176,)),
        ],
        compiler_params=pltpu.CompilerParams(
            collective_id=0, has_side_effects=True, vmem_limit_bytes=62 * 2**20
        ),
        name="block",
    )(tokens, out_grad, gate_weight.T, up_weight.T, down_weight)
    output, input_grad, gate_t, up_t, down_grad = pl.pallas_call(
        store,
        out_shape=(small, small, large, large, large),
        in_specs=[any_spec] * 5,
        out_specs=(hbm_spec,) * 5,
        scratch_shapes=[pltpu.VMEM(r.shape, BF) for r in results] + [pltpu.SemaphoreType.DMA((10,))],
        compiler_params=pltpu.CompilerParams(vmem_limit_bytes=62 * 2**20),
        name="store",
    )(*results)
    return output, input_grad, gate_t.T, up_t.T, down_grad


def solution(mesh):
    placed = (
        P(("dp", "gx", "gy"), "gz"),
        P("gz", ("gx", "gy")),
        P("gz", ("gx", "gy")),
        P(("gx", "gy"), "gz"),
        P(("dp", "gx", "gy"), "gz"),
    )
    return jax.shard_map(
        body,
        mesh=mesh,
        in_specs=placed,
        out_specs=(
            P(("dp", "gx", "gy"), "gz"),
            P(("dp", "gx", "gy"), "gz"),
            P("gz", ("gx", "gy")),
            P("gz", ("gx", "gy")),
            P(("gx", "gy"), "gz"),
        ),
        check_vma=False,
    )
```

time: 92.1 us -> 82.8 us (0.90)
  local copies, waits for them, and re-layouts: 8.03 us -> 0 us
  Pallas kernels: 83 us -> 81.9 us
    unnamed x15 -> x0, local copies, waits for them, and re-layouts: 8.03 us -> none
    pallas_call x1, Pallas kernels: 83 us -> 79.6 us  [body(): pl.pallas_call(kernel, out_shape=(small, small, large, large, large), in_...]
    pallas_call x0 -> x1, Pallas kernels: none -> 2.23 us  [body(): pl.pallas_call(store, out_shape=(small, small, large, large, large), in_s...]
where the time goes in v2:
time: 82.8 us; the launch traced here: 82.5 us
  Pallas kernels  81.9 us (99%)
    pallas_call x1, Pallas kernels, body(): pl.pallas_call(kernel, out_shape=(small, small, large, large, large), in_...  79.6 us
    pallas_call x1, Pallas kernels, body(): pl.pallas_call(store, out_shape=(small, small, large, large, large), in_s...  2.23 us

profile of v2, /device:TPU:1, one launch (start us, length us, event | category | flops | bytes accessed | tf_op | source)
XLA Modules:
  0.0 82.5 jit_solution(14505627453084295560)
XLA Ops:
  0.6 79.6 %block.1 = (bf16[16,512]{1,0:T(8,128)(2,1)}, bf16[16,512]{1,0:T(8,128)(2,1)}, bf16[464,512]{1,0:T(8,128)(2,1)}, bf16[464,512]{1,0:T(8,128)(2,1)}, bf16[464,512]{1,0:T(8,128)(2,1)}) custom-call(bf16[16,512]{1,0:T(8,128)(2,1)} %tok_ref.1, bf16[16,512]{1,0:T(8,128)(2,1)} %grad_ref.1, bf16[464,512]{1,0:T(8,128)(2,1)} %bitcast.4, bf16[464,512]{1,0:T(8,128)(2,1)} %bitcast.5, ...), custom_call_target="tpu_custom_call" | custom-call | tf_op jit(solution)/shard_map/block/pallas_call | solution.py:315
  80.3 2.2 %store.1 = (bf16[16,512]{1,0:T(8,128)(2,1)}, bf16[16,512]{1,0:T(8,128)(2,1)}, bf16[464,512]{1,0:T(8,128)(2,1)}, bf16[464,512]{1,0:T(8,128)(2,1)}, bf16[464,512]{1,0:T(8,128)(2,1)}) custom-call(bf16[16,512]{1,0:T(8,128)(2,1)} %get-tuple-element.15.refs_0_, bf16[16,512]{1,0:T(8,128)(2,1)} %get-tuple-element.16.refs_1_, ...), custom_call_target="tpu_custom_call" | custom-call | tf_op jit(solution)/shard_map/store/pallas_call | solution.py:346

commit v3 on v2

--- a/solution.py
+++ b/solution.py
@@ -89,26 +89,28 @@
         copy.wait()
     pl.semaphore_wait(barrier, len(partners))
 
-    def ysends(a, d, whole):
-        ref = T.at[a, d, gx] if whole else T.at[a, d, gx, gy]
+    def ysends(a, d):
+        ref = T.at[a, d, gx, gy]
         return {k: send(ref, ref, ydev(k)) for k in FAR}
 
     def xsends(ref):
         return [send(ref, ref, xdev(k)) for k in (2, 1, 3)]
 
-    tok_y = ysends(0, dp, False)
-    tok_x = xsends(T.at[0, dp, gx, gy])
-    grad_x = xsends(T.at[1, dp, gx, gy])
-    swap = [send(T.at[a, dp, gx, gy], T.at[a, dp, gx, gy], partner) for a in range(2)]
+    def pass_on(a):
+        for k in (1, 7, 2, 6, 3, 5, 4):
+            ys[a][k].wait_recv()
+            xs[a] += xsends(T.at[a, dp, lax.rem(gx + 8 - k, 8), gy])
+
+    ys, xs = {}, {}
+    ys[0] = ysends(0, dp)
+    xs[0] = xsends(T.at[0, dp, gx, gy])
+    ys[1] = ysends(1, dp)
     for copy in w_in:
         copy.wait()
-    for k in (1, 7, 2, 6, 3, 5, 4):
-        tok_y[k].wait_recv()
-        tok_x += xsends(T.at[0, dp, lax.rem(gx + 8 - k, 8), gy])
-        if k == 7:
-            arrive(grad_x)
-            grad_y = ysends(1, dp, True)
-    arrive(tok_x)
+    pass_on(0)
+    xs[1] = xsends(T.at[1, dp, gx, gy])
+    swap = [send(T.at[a, dp, gx, gy], T.at[a, dp, gx, gy], partner) for a in range(2)]
+    arrive(xs[0])
 
     def project(q, x):
         far = lax.dot_general(W[q, other], x, NT, preferred_element_type=F32)
@@ -159,46 +161,58 @@
     up_c = project(1, x)
     gate_z = scatter(0, gate_c)
     up_z = scatter(1, up_c)
+    pass_on(1)
     arrive(swap)
-    other_y = ysends(0, odp, False)
-    other_x = xsends(T.at[1, odp, gx, gy])
+    other_y = [copy for a in range(2) for copy in ysends(a, odp).values()]
     relay(0, gate_z)
     relay(1, up_z)
-    arrive(grad_y.values())
+    arrive(xs[1])
     hg_c = project(2, T[1, dp].reshape(512, 512))
     hg_z = scatter(2, hg_c)
-    arrive(other_x)
-    other_x = list(ysends(1, odp, True).values())
-    arrive(other_y.values())
-    other_y = xsends(T.at[0, odp, :, gy])
-    relay(2, hg_z)
+    arrive(other_y)
+    other_x = [copy for a in range(2) for copy in xsends(T.at[a, odp, :, gy])]
 
     right, left, to_core = {}, {}, {}
+    near_b = zdev(2 * dp - 1)
 
     def spread(q, value):
-        D[q, c, z] = value.astype(BF)
-        ref = D.at[q, c, z]
-        right[q] = send(ref, ref, zdev(1))
-        left[q] = send(ref, ref, zdev(-1))
+        D[q, dp, c, zh] = value.astype(BF)
+        ref = D.at[q, dp, c, zh]
+        right[q] = send(ref, ref, zdev(2))
+        left[q] = send(ref, ref, zdev(-2))
         to_core[q] = [send(ref, ref, core)]
 
-    def step(q, s):
-        there, back = lax.rem(z + 8 - s, 8), lax.rem(z + s, 8)
-        a, b = D.at[q, c, there], D.at[q, c, back]
+    def spread_on(q):
+        there, back = lax.rem(zh + 3, 4), lax.rem(zh + 1, 4)
         right[q].wait_recv()
-        if s < 4:
-            a_next = a if s < 3 else D.at[q, c, there, low]
-            right[q] = send(a_next, a_next, zdev(1))
-            to_core[q].append(send(a, a, core))
+        ref = D.at[q, dp, c, there, low]
+        right[q] = send(ref, ref, zdev(2))
+        ref = D.at[q, dp, c, there]
+        to_core[q].append(send(ref, ref, core))
         left[q].wait_recv()
-        if s < 4:
-            b_next = b if s < 3 else D.at[q, c, back, high]
-            left[q] = send(b_next, b_next, zdev(-1))
-        to_core[q].append(send(b, b, core))
+        ref = D.at[q, dp, c, back, high]
+        left[q] = send(ref, ref, zdev(-2))
+        ref = D.at[q, dp, c, back]
+        to_core[q].append(send(ref, ref, core))
+
+    def spread_end(q):
+        right[q].wait_recv()
+        left[q].wait_recv()
+        ref = D.at[q, dp, c, lax.rem(zh + 2, 4)]
+        to_core[q].append(send(ref, ref, core))
+
+    def swap_replicas(q):
+        refs = [D.at[q, dp, c, lax.rem(zh + 4 + k, 4)] for k in (0, 2 * dp - 1, 1 - 2 * dp)]
+        return [
+            send(refs[0], refs[0], partner),
+            send(refs[0], refs[0], near_b),
+            send(refs[1], refs[1], partner),
+            send(refs[2], refs[2], near_b),
+        ]
 
     def rows(q, d):
         halves = [
-            jnp.concatenate([D[q, h, 2 * j + d] for j in range(4)], axis=1) for h in range(2)
+            jnp.concatenate([D[q, d, h, j] for j in range(4)], axis=1) for h in range(2)
         ]
         return jnp.concatenate(halves, axis=0)
 
@@ -240,24 +254,20 @@
     V[0] = up_val * gate_sig * (1.0 + gate_val * (1.0 - gate_sig))
     V[1] = gate_act
     spread(0, gate_act * up_val)
-    step(0, 1)
+    relay(2, hg_z)
+    spread_on(0)
     hid_grad = total(2, hg_z)
     spread(1, hid_grad * V[0])
     spread(2, hid_grad * V[1])
-    step(0, 2)
-    step(1, 1)
-    step(2, 1)
-    step(0, 3)
-    step(1, 2)
-    step(2, 2)
-    step(0, 4)
-    step(1, 3)
-    step(2, 3)
+    spread_end(0)
     arrive(to_core[0])
     part = lax.dot_general(rows(0, dp), W[2].reshape(480, 512), TN, preferred_element_type=F32)
     out_x = x_scatter(0, part)
-    step(1, 4)
-    step(2, 4)
+    spread_on(1)
+    spread_on(2)
+    swapped = [swap_replicas(q) for q in range(3)]
+    spread_end(1)
+    spread_end(2)
     arrive(to_core[1])
     arrive(to_core[2])
     both = jnp.concatenate([rows(1, dp), rows(2, dp)], axis=0)
@@ -270,7 +280,7 @@
     def weight_grad(q, ref):
         right = T[1 if q == 0 else 0].reshape(1024, 512)
         for h in range(2):
-            left = jnp.concatenate([D[q, h, 2 * j + d] for d in range(2) for j in range(4)], axis=1)
+            left = jnp.concatenate([D[q, d, h, j] for d in range(2) for j in range(4)], axis=1)
             value = lax.dot_general(left, right, NN, preferred_element_type=F32).astype(BF)
             if h == 0:
                 WG[q, 0:HALF] = value
@@ -278,13 +288,17 @@
                 WG[q, HALF : HALF + LAST] = value[0:LAST]
         done.append(local(WG.at[q], ref))
 
-    arrive(other_y)
-    arrive(other_x)
-    weight_grad(0, dg_ref)
     in_y = y_scatter(1, 0, in_x)
     in_y += y_scatter(1, 1, in_x)
-    weight_grad(1, gg_ref)
-    weight_grad(2, ug_ref)
+    late = []
+    for q in range(3):
+        arrive(swapped[q])
+        ref = D.at[q, odp, c]
+        late.append(send(ref, ref, core))
+    arrive(other_x)
+    for q, ref in enumerate((dg_ref, gg_ref, ug_ref)):
+        arrive([late[q]])
+        weight_grad(q, ref)
     done.append(finish(0, out_y, out_ref))
     done.append(finish(1, in_y, ing_ref))
     for copy in sent:
@@ -295,14 +309,21 @@
 
 def store(*refs):
     n = (len(refs) - 1) // 3
-    held, sem = refs[2 * n : 3 * n], refs[-1]
-    fetch = [pltpu.make_async_copy(refs[i], held[i], sem.at[i]) for i in range(n)]
-    put = [pltpu.make_async_copy(held[i], refs[n + i], sem.at[n + i]) for i in range(n)]
+    sem = refs[-1]
+    fetch, put = [], []
+    for i in range(n):
+        source, result, held = refs[i], refs[n + i], refs[2 * n + i]
+        size = source.shape[0]
+        cuts = [0, 160, 320, size] if size > 160 else [0, size]
+        for start, stop in zip(cuts[:-1], cuts[1:], strict=True):
+            rows, k = pl.ds(start, stop - start), len(fetch)
+            fetch.append(pltpu.make_async_copy(source.at[rows], held.at[rows], sem.at[0, k]))
+            put.append(pltpu.make_async_copy(held.at[rows], result.at[rows], sem.at[1, k]))
     for copy in fetch:
         copy.start()
-    for i in range(n):
-        fetch[i].wait()
-        put[i].start()
+    for into, out in zip(fetch, put, strict=True):
+        into.wait()
+        out.start()
     for copy in put:
         copy.wait()
 
@@ -327,7 +348,7 @@
             pltpu.VMEM((3, HALF, 128), BF),
             pltpu.VMEM((3, 2, HALF, 128), BF),
             pltpu.VMEM((2, HALF, 128), F32),
-            pltpu.VMEM((3, 2, 8, HALF, 128), BF),
+            pltpu.VMEM((3, 2, 2, 4, HALF, 128), BF),
             pltpu.VMEM((2, 8, 4, 16, 512), BF),
             pltpu.VMEM((2, 3, 8, 16, 512), BF),
             pltpu.VMEM((2, 8, 16, 512), BF),
@@ -335,8 +356,8 @@
             pltpu.VMEM((3, 464, 512), BF),
             pltpu.VMEM((2, 16, 512), BF),
             pltpu.SemaphoreType.DMA((16,)),
-            pltpu.SemaphoreType.DMA((176,)),
-            pltpu.SemaphoreType.DMA((176,)),
+            pltpu.SemaphoreType.DMA((208,)),
+            pltpu.SemaphoreType.DMA((208,)),
         ],
         compiler_params=pltpu.CompilerParams(
             collective_id=0, has_side_effects=True, vmem_limit_bytes=62 * 2**20
@@ -348,7 +369,7 @@
         out_shape=(small, small, large, large, large),
         in_specs=[any_spec] * 5,
         out_specs=(hbm_spec,) * 5,
-        scratch_shapes=[pltpu.VMEM(r.shape, BF) for r in results] + [pltpu.SemaphoreType.DMA((10,))],
+        scratch_shapes=[pltpu.VMEM(r.shape, BF) for r in results] + [pltpu.SemaphoreType.DMA((2, 11))],
         compiler_params=pltpu.CompilerParams(vmem_limit_bytes=62 * 2**20),
         name="store",
     )(*results)

time: 82.8 us -> 81.4 us (0.983)
  Pallas kernels: 81.9 us -> 80.5 us
    pallas_call x1, Pallas kernels: 79.6 us -> 78.1 us  [body(): pl.pallas_call(kernel, out_shape=(small, small, large, large, large), in_...]
where the time goes in v3:
time: 81.4 us; the launch traced here: 81.1 us
  Pallas kernels  80.5 us (99%)
    pallas_call x1, Pallas kernels, body(): pl.pallas_call(kernel, out_shape=(small, small, large, large, large), in_...  78.1 us
    pallas_call x1, Pallas kernels, body(): pl.pallas_call(store, out_shape=(small, small, large, large, large), in_s...  2.32 us

profile of v3, /device:TPU:1, one launch (start us, length us, event | category | flops | bytes accessed | tf_op | source)
XLA Modules:
  0.0 81.1 jit_solution(12595120676125771112)
XLA Ops:
  0.6 78.1 %block.1 = (bf16[16,512]{1,0:T(8,128)(2,1)}, bf16[16,512]{1,0:T(8,128)(2,1)}, bf16[464,512]{1,0:T(8,128)(2,1)}, bf16[464,512]{1,0:T(8,128)(2,1)}, bf16[464,512]{1,0:T(8,128)(2,1)}) custom-call(bf16[16,512]{1,0:T(8,128)(2,1)} %tok_ref.1, bf16[16,512]{1,0:T(8,128)(2,1)} %grad_ref.1, bf16[464,512]{1,0:T(8,128)(2,1)} %bitcast.4, bf16[464,512]{1,0:T(8,128)(2,1)} %bitcast.5, ...), custom_call_target="tpu_custom_call" | custom-call | tf_op jit(solution)/shard_map/block/pallas_call | solution.py:336
  78.8 2.3 %store.1 = (bf16[16,512]{1,0:T(8,128)(2,1)}, bf16[16,512]{1,0:T(8,128)(2,1)}, bf16[464,512]{1,0:T(8,128)(2,1)}, bf16[464,512]{1,0:T(8,128)(2,1)}, bf16[464,512]{1,0:T(8,128)(2,1)}) custom-call(bf16[16,512]{1,0:T(8,128)(2,1)} %get-tuple-element.15.refs_0_, bf16[16,512]{1,0:T(8,128)(2,1)} %get-tuple-element.16.refs_1_, ...), custom_call_target="tpu_custom_call" | custom-call | tf_op jit(solution)/shard_map/store/pallas_call | solution.py:367

commit v4 on v3

--- a/solution.py
+++ b/solution.py
@@ -221,8 +221,8 @@
         for g in range(8):
             OB[o, lax.rem(g + 14 - gx, 8)] = part[g]
         groups = []
-        for h in range(2):
-            block = pl.ds(4 * h, 4)
+        for h in range(4):
+            block = pl.ds(2 * h, 2)
             groups.append([
                 send(OB.at[o, block, lax.rem(gy + k, 4)], RX.at[o, k - 1, block], xdev(k))
                 for k in (2, 1, 3)
@@ -231,12 +231,12 @@
 
     def y_scatter(o, h, copies):
         arrive(copies[h])
-        block = slice(4 * h, 4 * h + 4)
+        block = slice(2 * h, 2 * h + 2)
         value = OB[o, block, gy].astype(F32)
         for k in range(3):
             value = value + RX[o, k, block].astype(F32)
         SY[o, block] = value.astype(BF)
-        order = (2, 1, 3, 0) if h == 0 else (4, 5, 7)
+        order = ((1, 0), (2, 3), (4, 5), (7,))[h]
         return [send(SY.at[o, i], RY.at[o, (i + 2) % 8 - 1], ydev((i + 2) % 8)) for i in order]
 
     def finish(o, copies, ref):
@@ -273,7 +273,7 @@
     both = jnp.concatenate([rows(1, dp), rows(2, dp)], axis=0)
     part = lax.dot_general(both, W[0:2].reshape(960, 512), TN, preferred_element_type=F32)
     in_x = x_scatter(1, part)
-    out_y = y_scatter(0, 0, out_x) + y_scatter(0, 1, out_x)
+    out_y = [copy for h in range(4) for copy in y_scatter(0, h, out_x)]
 
     done = []
 
@@ -288,8 +288,7 @@
                 WG[q, HALF : HALF + LAST] = value[0:LAST]
         done.append(local(WG.at[q], ref))
 
-    in_y = y_scatter(1, 0, in_x)
-    in_y += y_scatter(1, 1, in_x)
+    in_y = [copy for h in range(4) for copy in y_scatter(1, h, in_x)]
     late = []
     for q in range(3):
         arrive(swapped[q])
@@ -356,8 +355,8 @@
             pltpu.VMEM((3, 464, 512), BF),
             pltpu.VMEM((2, 16, 512), BF),
             pltpu.SemaphoreType.DMA((16,)),
-            pltpu.SemaphoreType.DMA((208,)),
-            pltpu.SemaphoreType.DMA((208,)),
+            pltpu.SemaphoreType.DMA((224,)),
+            pltpu.SemaphoreType.DMA((224,)),
         ],
         compiler_params=pltpu.CompilerParams(
             collective_id=0, has_side_effects=True, vmem_limit_bytes=62 * 2**20

time: 81.4 us -> 81.7 us (level)
  no operation moved by 1% of the time
where the time goes in v4:
time: 81.7 us; the launch traced here: 81.3 us
  Pallas kernels  80.7 us (99%)
    pallas_call x1, Pallas kernels, body(): pl.pallas_call(kernel, out_shape=(small, small, large, large, large), in_...  78.4 us
    pallas_call x1, Pallas kernels, body(): pl.pallas_call(store, out_shape=(small, small, large, large, large), in_s...  2.32 us

profile of v4, /device:TPU:1, one launch (start us, length us, event | category | flops | bytes accessed | tf_op | source)
XLA Modules:
  0.0 81.3 jit_solution(10044653516131980973)
XLA Ops:
  0.6 78.4 %block.1 = (bf16[16,512]{1,0:T(8,128)(2,1)}, bf16[16,512]{1,0:T(8,128)(2,1)}, bf16[464,512]{1,0:T(8,128)(2,1)}, bf16[464,512]{1,0:T(8,128)(2,1)}, bf16[464,512]{1,0:T(8,128)(2,1)}) custom-call(bf16[16,512]{1,0:T(8,128)(2,1)} %tok_ref.1, bf16[16,512]{1,0:T(8,128)(2,1)} %grad_ref.1, bf16[464,512]{1,0:T(8,128)(2,1)} %bitcast.4, bf16[464,512]{1,0:T(8,128)(2,1)} %bitcast.5, ...), custom_call_target="tpu_custom_call" | custom-call | tf_op jit(solution)/shard_map/block/pallas_call | solution.py:335
  79.0 2.3 %store.1 = (bf16[16,512]{1,0:T(8,128)(2,1)}, bf16[16,512]{1,0:T(8,128)(2,1)}, bf16[464,512]{1,0:T(8,128)(2,1)}, bf16[464,512]{1,0:T(8,128)(2,1)}, bf16[464,512]{1,0:T(8,128)(2,1)}) custom-call(bf16[16,512]{1,0:T(8,128)(2,1)} %get-tuple-element.15.refs_0_, bf16[16,512]{1,0:T(8,128)(2,1)} %get-tuple-element.16.refs_1_, ...), custom_call_target="tpu_custom_call" | custom-call | tf_op jit(solution)/shard_map/store/pallas_call | solution.py:366
